TPU v7x, 512 devices: a whole 4x8x8 slice. The times are simulated.
512 devices in a mesh: ctx: 64 (over z, y), fsdp: 8 (over x, core).
Axes of the slice: x: 4, y: 8, z: 8, core: 2. Of those that a mesh axis runs over, the one named last changes fastest.
Arguments:
- tokens: bfloat16 [32768, 4608], P('ctx'), may hold values from -40 to 40
- w_query: bfloat16 [4608, 2048], P('ctx', 'fsdp'), may hold values from -0.1 to 0.1
- w_key: bfloat16 [4608, 1024], P('ctx', 'fsdp'), may hold values from -0.1 to 0.1
- w_value: bfloat16 [4608, 1024], P('ctx', 'fsdp'), may hold values from -0.09375 to 0.09375
- doc_ids: int32 [32768], replicated, may hold values from 0 to 15, never falling along the last dimension, each value on 1 to 8192 neighbouring positions
Outputs:
- attended: bfloat16 [32768, 2048], P(('ctx', 'fsdp'))
Inputs may be any that keep to these rules, and one draw needn't show every extreme that they name: `doc_ids`: document numbers start at 0, never fall along the sequence, and each document spans 1 to 8192 consecutive positions; one spans exactly 8192.
All inputs are finite; a program needn't handle non-finite values.
Results may differ from a plain program's by a relative error of at most 0.007.
Values may be sent and summed in bfloat16 or wider, within the bound.
A program may use at most 64 MiB of HBM per device.

v0:
```python
import jax
import jax.numpy as jnp
from jax import lax
from jax.sharding import PartitionSpec as P

HD = 128
WINDOW = 4096


query_scale = 144.0 ** (-0.5)
score_cap = 50.0


def passed_along(shard, axis, by):
    count = lax.axis_size(axis)
    pairs = [(i, i + by) for i in range(count) if 0 <= i + by < count]
    return lax.ppermute(shard, axis, pairs)


def fetch_halo(keyval, shard_rows):
    blocks_back = WINDOW // shard_rows
    collected = []
    for offset in range(blocks_back, 0, -1):
        collected.append(passed_along(keyval, "ctx", offset))
    return jnp.concatenate(collected, axis=0)


def attend(queries, keyval, earlier, doc_ids, shard_rows):
    shard_index = lax.axis_index("ctx")
    blocks_back = earlier.shape[0] // shard_rows
    heads_kv = keyval.shape[1] // (2 * HD)
    group_size = queries.shape[1] // (HD * heads_kv)
    query_heads = queries.reshape(shard_rows, heads_kv, group_size, HD)
    row_offsets = jnp.arange(shard_rows, dtype=jnp.int32)
    query_pos = shard_index * shard_rows + row_offsets
    query_doc = lax.dynamic_slice_in_dim(doc_ids, shard_index * shard_rows, shard_rows, 0)
    last_pos = doc_ids.shape[0] - 1

    def tile_mask(key_pos):
        key_doc = jnp.take(doc_ids, jnp.clip(key_pos, 0, last_pos))
        distance = query_pos[:, None] - key_pos[None, :]
        return (
            (query_doc[:, None] == key_doc[None, :])
            & (distance >= 0)
            & (distance < WINDOW)
            & (key_pos[None, :] >= 0)
        )

    def update(carry_state, kv_tile, visible):
        denom, total_sum = carry_state
        key_tile = kv_tile[:, : heads_kv * HD].reshape(shard_rows, heads_kv, HD)
        value_tile = kv_tile[:, heads_kv * HD :].reshape(shard_rows, heads_kv, HD)
        scores = (
            jnp.einsum("cngd,lnd->ngcl", query_heads, key_tile, preferred_element_type=jnp.float32)
            * query_scale
        )
        scores = score_cap * jnp.tanh(scores / score_cap)
        weights_exp = jnp.where(visible, jnp.exp(scores), 0.0)
        denom = denom + jnp.sum(weights_exp, axis=-1)
        product = jnp.einsum(
            "ngcl,lnd->ngcd",
            weights_exp.astype(jnp.bfloat16),
            value_tile,
            preferred_element_type=jnp.float32,
        )
        return (denom, total_sum + product)

    start_state = (
        jnp.zeros((heads_kv, group_size, shard_rows), jnp.float32),
        jnp.zeros((heads_kv, group_size, shard_rows, HD), jnp.float32),
    )
    carry_state = update(start_state, keyval, tile_mask(query_pos))

    def halo_step(tile_index, carry_state):
        kv_tile = lax.dynamic_slice_in_dim(earlier, tile_index * shard_rows, shard_rows, 0)
        key_pos = (shard_index - blocks_back + tile_index) * shard_rows + row_offsets
        visible = tile_mask(key_pos)
        return update(carry_state, kv_tile, visible)

    denom, total_sum = lax.fori_loop(0, blocks_back, halo_step, carry_state)
    result = total_sum / denom[..., None]
    return (
        result.transpose(2, 0, 1, 3)
        .reshape(shard_rows, heads_kv * group_size * HD)
        .astype(jnp.bfloat16)
    )


def on_device(tokens, w_query, w_key, w_value, doc_ids):
    shard_rows = tokens.shape[0]
    pieces = (
        lax.all_gather(w_query, "ctx", axis=0, tiled=True),
        lax.all_gather(w_key, "ctx", axis=0, tiled=True),
        lax.all_gather(w_value, "ctx", axis=0, tiled=True),
    )
    query_sum, key_sum, value_sum = tuple(
        (jnp.dot(tokens, piece, preferred_element_type=jnp.float32) for piece in pieces)
    )
    keyval = jnp.concatenate([key_sum.astype(jnp.bfloat16), value_sum.astype(jnp.bfloat16)], axis=1)
    earlier = fetch_halo(keyval, shard_rows)
    queries = query_sum.astype(jnp.bfloat16)
    head_results = attend(queries, keyval, earlier, doc_ids, shard_rows)
    return lax.all_to_all(head_results, "fsdp", split_axis=0, concat_axis=1, tiled=True)


def solution(mesh):
    return jax.shard_map(
        on_device,
        mesh=mesh,
        in_specs=(P("ctx", None), P("ctx", "fsdp"), P("ctx", "fsdp"), P("ctx", "fsdp"), P()),
        out_specs=P(("ctx", "fsdp"), None),
        check_vma=False,
    )
```

profile of v0, /device:TPU:1, one launch (start us, length us, event | category | flops | bytes accessed | tf_op | source)
XLA Modules:
  0.0 365.8 jit_solution(7889690878025429960)
XLA Ops:
  8.8 3.6 gather_fusion.1
  12.4 81.5 %all-gather.8.cloned.1.call-done = bf16[4608,128]{1,0:T(8,128)(2,1)} async-done(((bf16[72,128]{1,0:T(8,128)(2,1)}), bf16[4608,128]{1,0:T(8,128)(2,1)}) %all-gather.8.cloned.1.call-update) | async-done | bytes 1179664 | tf_op jit(solution)/shard_map/all_gather | solution.py:94
  93.9 4.4 %convolution_convert_fusion.1 = bf16[512,128]{0,1:T(8,128)(2,1)S(1)} fusion(bf16[512,4608]{1,0:T(8,128)(2,1)} %param.9, bf16[4608,128]{1,0:T(8,128)(2,1)} %all-gather.8.cloned.1.call-done), kind=kOutput, calls=%fused_computation.30 | convolution fusion | flops 604045312 | bytes 6029312 | tf_op jit(solution)/shard_map/dot_general | solution.py:97
  98.3 77.7 %all-gather.4.cloned.1.call-done = bf16[4608,128]{1,0:T(8,128)(2,1)} async-done(((bf16[72,128]{1,0:T(8,128)(2,1)}), bf16[4608,128]{1,0:T(8,128)(2,1)}) %all-gather.4.cloned.1.call-update) | async-done | bytes 1179664 | tf_op jit(solution)/shard_map/all_gather | solution.py:93
  176.0 4.4 %convolution_convert_fusion.2 = bf16[512,128]{0,1:T(8,128)(2,1)S(1)} fusion(bf16[512,4608]{1,0:T(8,128)(2,1)} %param.9, bf16[4608,128]{1,0:T(8,128)(2,1)} %all-gather.4.cloned.1.call-done), kind=kOutput, calls=%fused_computation.31 | convolution fusion | flops 604045312 | bytes 6029312 | tf_op jit(solution)/shard_map/dot_general | solution.py:97
  180.4 2.6 collective-permute-start
  183.2 2.7 collective-permute-start.1
  185.8 4.8 %collective-permute-start.2 = (bf16[512,256]{0,1:T(8,128)(2,1)S(1)}, bf16[512,256]{0,1:T(8,128)(2,1)S(1)}, u32[]{:S(2)}, u32[]{:S(2)}) collective-permute-start(bf16[512,256]{0,1:T(8,128)(2,1)S(1)} %pad_maximum_fusion), channel_id=1, source_target_pairs={{0,48},{8,56},{16,64},{24,72},{32,80},{40,88},{48,96},{56,104},{64... | collective-permute-start | bytes 786440 | tf_op jit(solution)/shard_map/ppermute | solution.py:17
  191.0 5.4 %collective-permute-start.3 = (bf16[512,256]{0,1:T(8,128)(2,1)S(1)}, bf16[512,256]{0,1:T(8,128)(2,1)S(1)}, u32[]{:S(2)}, u32[]{:S(2)}) collective-permute-start(bf16[512,256]{0,1:T(8,128)(2,1)S(1)} %pad_maximum_fusion), channel_id=1, source_target_pairs={{0,40},{8,48},{16,56},{24,64},{32,72},{40,80},{48,88},{56,96},{64,... | collective-permute-start | bytes 786440 | tf_op jit(solution)/shard_map/ppermute | solution.py:17
  196.5 3.9 %collective-permute-start.4 = (bf16[512,256]{0,1:T(8,128)(2,1)S(1)}, bf16[512,256]{0,1:T(8,128)(2,1)S(1)}, u32[]{:S(2)}, u32[]{:S(2)}) collective-permute-start(bf16[512,256]{0,1:T(8,128)(2,1)S(1)} %pad_maximum_fusion), channel_id=1, source_target_pairs={{0,32},{8,40},{16,48},{24,56},{32,64},{40,72},{48,80},{56,88},{64,... | collective-permute-start | bytes 786440 | tf_op jit(solution)/shard_map/ppermute | solution.py:17
  200.4 4.1 %collective-permute-start.5 = (bf16[512,256]{0,1:T(8,128)(2,1)S(1)}, bf16[512,256]{0,1:T(8,128)(2,1)S(1)}, u32[]{:S(2)}, u32[]{:S(2)}) collective-permute-start(bf16[512,256]{0,1:T(8,128)(2,1)S(1)} %pad_maximum_fusion), channel_id=1, source_target_pairs={{0,24},{8,32},{16,40},{24,48},{32,56},{40,64},{48,72},{56,80},{64,... | collective-permute-start | bytes 786440 | tf_op jit(solution)/shard_map/ppermute | solution.py:17
  205.3 5.2 %collective-permute-start.6 = (bf16[512,256]{0,1:T(8,128)(2,1)S(1)}, bf16[512,256]{0,1:T(8,128)(2,1)S(1)}, u32[]{:S(2)}, u32[]{:S(2)}) collective-permute-start(bf16[512,256]{0,1:T(8,128)(2,1)S(1)} %pad_maximum_fusion), channel_id=1, source_target_pairs={{0,16},{8,24},{16,32},{24,40},{32,48},{40,56},{48,64},{56,72},{64,... | collective-permute-start | bytes 786440 | tf_op jit(solution)/shard_map/ppermute | solution.py:17
  214.8 2.0 collective-permute-done.5
  217.5 8.7 %collective-permute-done.6 = bf16[512,256]{0,1:T(8,128)(2,1)S(1)} collective-permute-done((bf16[512,256]{0,1:T(8,128)(2,1)S(1)}, bf16[512,256]{0,1:T(8,128)(2,1)S(1)}, u32[]{:S(2)}, u32[]{:S(2)}) %collective-permute-start.6) | collective-permute-done | bytes 262176 | tf_op jit(solution)/shard_map/ppermute | solution.py:17
  227.0 15.6 %collective-permute-done.7 = bf16[512,256]{0,1:T(8,128)(2,1)S(1)} collective-permute-done((bf16[512,256]{0,1:T(8,128)(2,1)S(1)}, bf16[512,256]{0,1:T(8,128)(2,1)S(1)}, u32[]{:S(2)}, u32[]{:S(2)}) %collective-permute-start.7) | collective-permute-done | bytes 262176 | tf_op jit(solution)/shard_map/ppermute | solution.py:17
  243.3 38.2 %all-gather.6.cloned.1.call-done = bf16[4608,256]{1,0:T(8,128)(2,1)} async-done(((bf16[72,256]{1,0:T(8,128)(2,1)}), bf16[4608,256]{1,0:T(8,128)(2,1)}) %all-gather.6.cloned.1.call-update) | async-done | bytes 2359312 | tf_op jit(solution)/shard_map/all_gather | solution.py:92
  281.5 4.5 %convolution_convert_fusion = bf16[512,256]{0,1:T(8,128)(2,1)S(1)} fusion(bf16[512,4608]{1,0:T(8,128)(2,1)} %param.9, bf16[4608,256]{1,0:T(8,128)(2,1)} %all-gather.6.cloned.1.call-done), kind=kOutput, calls=%fused_computation.29 | convolution fusion | flops 1208090624 | bytes 7340032 | tf_op jit(solution)/shard_map/dot_general | solution.py:97
  287.6 55.5 %while.18 = (s32[]{:T(128)}, f32[1,2,512]{2,1,0:T(2,128)S(1)}, f32[1,2,512,128]{3,2,1,0:T(8,128)S(1)}, s32[512]{0:T(512)S(1)}, s32[]{:T(128)}, /*index=5*/s32[32...) while((s32[]{:T(128)}, f32[1,2,512]{2,1,0:T(2,128)S(1)}, ...), condition=%wide.region_3.5_spmd.clone, body=%wide.region_1.4_spmd.clone.sunk | while | flops 273032704 | bytes 4242675 | solution.py:80
  287.7 3.1 gather_fusion
  291.3 1.8 fusion.39
  294.6 3.1 gather_fusion
  298.2 1.8 fusion.39
  301.6 3.1 gather_fusion
  308.5 3.1 gather_fusion
  312.1 1.8 fusion.39
  315.4 3.1 gather_fusion
  319.1 1.8 fusion.39
  322.4 3.1 gather_fusion
  329.3 3.1 gather_fusion
  336.3 3.1 gather_fusion
  339.9 1.8 fusion.39
  343.8 14.7 %all_to_all.16 = bf16[8,64,256]{2,1,0:T(8,128)(2,1)S(1)} all-to-all(bf16[8,64,256]{2,1,0:T(8,128)(2,1)S(1)} %convert_element_type.38), channel_id=1, replica_groups=mesh['ctx'=64,'fsdp'=8] {'fsdp'}, dimensions={0} | all-to-all | bytes 524288 | tf_op jit(solution)/shard_map/all_to_all | solution.py:103
  (103 shorter events, 33.6 us)
Async XLA Ops:
  6.5 87.3 %all-gather.8.cloned.1.call-start = ((), (), s32[]{:S(2)}) async-start(), calls=%async_computation.3 | async-start | bytes 1198080 | tf_op jit(solution)/shard_map/all_gather | solution.py:94
  7.3 168.8 %all-gather.4.cloned.1.call-start = ((), (), s32[]{:S(2)}) async-start(), calls=%async_computation.1 | async-start | bytes 1198080 | tf_op jit(solution)/shard_map/all_gather | solution.py:93
  8.0 273.5 %all-gather.6.cloned.1.call-start = ((), (), s32[]{:S(2)}) async-start(), calls=%async_computation.2 | async-start | bytes 2396160 | tf_op jit(solution)/shard_map/all_gather | solution.py:92
  98.3 84.8 %copy-start = (s32[32768]{0:T(1024)S(1)}, s32[32768]{0:T(1024)}, u32[]{:S(2)}) copy-start(s32[32768]{0:T(1024)} %param.13) | copy-start | bytes 393220
  180.4 20.0 %collective-permute-start = (bf16[512,256]{0,1:T(8,128)(2,1)S(1)}, bf16[512,256]{0,1:T(8,128)(2,1)S(1)}, u32[]{:S(2)}, u32[]{:S(2)}) collective-permute-start(bf16[512,256]{0,1:T(8,128)(2,1)S(1)} %pad_maximum_fusion), channel_id=1, source_target_pairs={{0,64},{8,72},{16,80},{24,88},{32,96},{40,104},{48,112},{56,120},{... | collective-permute-start | bytes 786440 | tf_op jit(solution)/shard_map/ppermute | solution.py:17
  183.2 22.1 %collective-permute-start.1 = (bf16[512,256]{0,1:T(8,128)(2,1)S(1)}, bf16[512,256]{0,1:T(8,128)(2,1)S(1)}, u32[]{:S(2)}, u32[]{:S(2)}) collective-permute-start(bf16[512,256]{0,1:T(8,128)(2,1)S(1)} %pad_maximum_fusion), channel_id=1, source_target_pairs={{0,56},{8,64},{16,72},{24,80},{32,88},{40,96},{48,104},{56,112},{6... | collective-permute-start | bytes 786440 | tf_op jit(solution)/shard_map/ppermute | solution.py:17
  185.8 25.4 %collective-permute-start.2 = (bf16[512,256]{0,1:T(8,128)(2,1)S(1)}, bf16[512,256]{0,1:T(8,128)(2,1)S(1)}, u32[]{:S(2)}, u32[]{:S(2)}) collective-permute-start(bf16[512,256]{0,1:T(8,128)(2,1)S(1)} %pad_maximum_fusion), channel_id=1, source_target_pairs={{0,48},{8,56},{16,64},{24,72},{32,80},{40,88},{48,96},{56,104},{64... | collective-permute-start | bytes 786440 | tf_op jit(solution)/shard_map/ppermute | solution.py:17
  191.0 22.3 %collective-permute-start.3 = (bf16[512,256]{0,1:T(8,128)(2,1)S(1)}, bf16[512,256]{0,1:T(8,128)(2,1)S(1)}, u32[]{:S(2)}, u32[]{:S(2)}) collective-permute-start(bf16[512,256]{0,1:T(8,128)(2,1)S(1)} %pad_maximum_fusion), channel_id=1, source_target_pairs={{0,40},{8,48},{16,56},{24,64},{32,72},{40,80},{48,88},{56,96},{64,... | collective-permute-start | bytes 786440 | tf_op jit(solution)/shard_map/ppermute | solution.py:17
  196.5 17.6 %collective-permute-start.4 = (bf16[512,256]{0,1:T(8,128)(2,1)S(1)}, bf16[512,256]{0,1:T(8,128)(2,1)S(1)}, u32[]{:S(2)}, u32[]{:S(2)}) collective-permute-start(bf16[512,256]{0,1:T(8,128)(2,1)S(1)} %pad_maximum_fusion), channel_id=1, source_target_pairs={{0,32},{8,40},{16,48},{24,56},{32,64},{40,72},{48,80},{56,88},{64,... | collective-permute-start | bytes 786440 | tf_op jit(solution)/shard_map/ppermute | solution.py:17
  200.4 16.3 %collective-permute-start.5 = (bf16[512,256]{0,1:T(8,128)(2,1)S(1)}, bf16[512,256]{0,1:T(8,128)(2,1)S(1)}, u32[]{:S(2)}, u32[]{:S(2)}) collective-permute-start(bf16[512,256]{0,1:T(8,128)(2,1)S(1)} %pad_maximum_fusion), channel_id=1, source_target_pairs={{0,24},{8,32},{16,40},{24,48},{32,56},{40,64},{48,72},{56,80},{64,... | collective-permute-start | bytes 786440 | tf_op jit(solution)/shard_map/ppermute | solution.py:17
  205.3 20.9 %collective-permute-start.6 = (bf16[512,256]{0,1:T(8,128)(2,1)S(1)}, bf16[512,256]{0,1:T(8,128)(2,1)S(1)}, u32[]{:S(2)}, u32[]{:S(2)}) collective-permute-start(bf16[512,256]{0,1:T(8,128)(2,1)S(1)} %pad_maximum_fusion), channel_id=1, source_target_pairs={{0,16},{8,24},{16,32},{24,40},{32,48},{40,56},{48,64},{56,72},{64,... | collective-permute-start | bytes 786440 | tf_op jit(solution)/shard_map/ppermute | solution.py:17
  211.3 31.3 %collective-permute-start.7 = (bf16[512,256]{0,1:T(8,128)(2,1)S(1)}, bf16[512,256]{0,1:T(8,128)(2,1)S(1)}, u32[]{:S(2)}, u32[]{:S(2)}) collective-permute-start(bf16[512,256]{0,1:T(8,128)(2,1)S(1)} %pad_maximum_fusion), channel_id=1, source_target_pairs={{0,8},{8,16},{16,24},{24,32},{32,40},{40,48},{48,56},{56,64},{64,7... | collective-permute-start | bytes 786440 | tf_op jit(solution)/shard_map/ppermute | solution.py:17
Sparse Core Ops, SparseCore 0:
  10.4 83.4 all-gather.7
  96.9 79.0 all-gather.3
  179.1 102.3 all-gather.5
where the time goes:
time: 366 us
  waiting for transfers between devices  226 us (62%)
  matrix products  40.7 us (11%)
  local copies, waits for them, and re-layouts  36.2 us (10%)
  starting transfers between devices  30.1 us (8%)
  blocking collectives  14.7 us (4%)
  between operations  13.3 us (4%)
  other arithmetic  4.33 us (1%)
    all_gather x1, waiting for transfers between devices, on_device(): lax.all_gather(w_value, 'ctx', axis=0, tiled=True)  81.5 us
    all_gather x1, waiting for transfers between devices, on_device(): lax.all_gather(w_key, 'ctx', axis=0, tiled=True)  77.7 us
    all_gather x1, waiting for transfers between devices, on_device(): lax.all_gather(w_query, 'ctx', axis=0, tiled=True)  38.2 us
    ppermute x8, starting transfers between devices, passed_along(): return lax.ppermute(shard, axis, pairs)  30 us
    gather x9, local copies, waits for them, and re-layouts, tile_mask(): key_doc = jnp.take(doc_ids, jnp.clip(key_pos, 0, last_pos))  28.7 us
    ppermute x8, waiting for transfers between devices, passed_along(): return lax.ppermute(shard, axis, pairs)  26.2 us
    dot_general x9, matrix products, update(): jnp.einsum('cngd,lnd->ngcl', query_heads, key_tile, preferred_element_typ...  15.3 us
    all_to_all x1, blocking collectives, on_device(): lax.all_to_all(head_results, 'fsdp', split_axis=0, concat_axis=1, tiled=T...  14.7 us
  transfers between devices with their start and end apart: 11, of which 6 were waited for; matrix products, arithmetic and copies ran while one was open for 5% of the time, Pallas kernels for 0%

commit v1 on v0

v1 whole, which is shorter than its diff:
```python
import functools
import math

import jax
import jax.numpy as jnp
from jax import lax
from jax.experimental import pallas as pl
from jax.experimental.pallas import tpu as pltpu
from jax.sharding import PartitionSpec as P

MESH = pl.DeviceIdType.MESH
HD = 128
WINDOW = 4096
SHARD = 512
D = 4608
SLAB = 72
NZ = NY = 8
NF = 8
BF = jnp.bfloat16
F32 = jnp.float32

query_scale = 144.0 ** (-0.5)
score_cap = 50.0
IN_SCALE = query_scale / score_cap
OUT_SCALE = score_cap * math.log2(math.e)


def kernel(tok_hbm, wq_hbm, wk_hbm, wv_hbm, doc_ref, out_ref,
           tok, wk, wv, wq, kvs, q, acc, oacc, dacc, lower, att,
           loc_sem, k1s, k1r, v1s, v1r, k2s, k2r, v2s, v2r, q1s, q1r, q2s, q2r,
           hzs, hs, hr, as_, ar):
    c = lax.axis_index("ctx")
    f = lax.axis_index("fsdp")
    z, y = c // NY, c % NY

    def at(zz, yy):
        return (lax.rem(zz + NZ, NZ) * NY + lax.rem(yy + NY, NY), f)

    def remote(src, dst, ssem, rsem, dev):
        return pltpu.make_async_remote_copy(
            src_ref=src, dst_ref=dst, send_sem=ssem, recv_sem=rsem,
            device_id=dev, device_id_type=MESH)

    sent = []

    def go(copy):
        copy.start()
        sent.append(copy)

    own_q0 = pltpu.make_async_copy(wq_hbm.at[:, pl.ds(0, HD)], wq.at[0, z, y], loc_sem.at[0])
    own_q1 = pltpu.make_async_copy(wq_hbm.at[:, pl.ds(HD, HD)], wq.at[1, z, y], loc_sem.at[1])
    own_k = pltpu.make_async_copy(wk_hbm, wk.at[z, y], loc_sem.at[2])
    own_v = pltpu.make_async_copy(wv_hbm, wv.at[y, z], loc_sem.at[3])
    own_tok = pltpu.make_async_copy(tok_hbm, tok, loc_sem.at[4])
    own_k.start()
    own_v.start()
    own_q0.start()
    own_q1.start()
    own_tok.start()

    bar = pltpu.get_barrier_semaphore()
    peers = [at(z, y + d) for d in range(1, NY)]
    peers += [at(z + d, y) for d in range(1, NZ)]
    peers += [(c, lax.rem(f + d, NF)) for d in range(1, NF)]
    for p in peers:
        pl.semaphore_signal(bar, inc=1, device_id=p, device_id_type=MESH)

    @pl.when(y == NY - 1)
    def _():
        pl.semaphore_signal(bar, inc=1, device_id=at(z + 1, 0), device_id_type=MESH)

    @pl.when(y == 0)
    def _():
        pl.semaphore_signal(bar, inc=1, device_id=at(z - 1, NY - 1), device_id_type=MESH)

    edge = jnp.where((y == 0) | (y == NY - 1), 1, 0)
    pl.semaphore_wait(bar, len(peers) + edge)

    own_k.wait()
    own_v.wait()
    order = [1, 7, 2, 6, 3, 5, 4]
    for d in order:
        go(remote(wk.at[z, y], wk.at[z, y], k1s.at[d], k1r.at[d], at(z, y + d)))
        go(remote(wv.at[y, z], wv.at[y, z], v1s.at[d], v1r.at[d], at(z + d, y)))
    own_q0.wait()
    own_q1.wait()

    def q_first(s):
        for side in (0, 1):
            sign = 1 - 2 * side
            if s > (4 if side == 0 else 3):
                continue
            src = lax.rem(y - sign * (s - 1) + NY, NY)
            if s > 1:
                remote(wq.at[:, z, src], wq.at[:, z, src], q1s.at[side, s - 1], q1r.at[side, s - 1], at(z, y)).wait_recv()
            go(remote(wq.at[:, z, src], wq.at[:, z, src], q1s.at[side, s], q1r.at[side, s], at(z, y + sign)))

    def q_first_done():
        for side, s in ((0, 4), (1, 3)):
            sign = 1 - 2 * side
            src = lax.rem(y - sign * s + NY, NY)
            remote(wq.at[:, z, src], wq.at[:, z, src], q1s.at[side, s], q1r.at[side, s], at(z, y)).wait_recv()

    docs = doc_ref[...]
    half = doc_ref[pl.ds(pl.multiple_of((c // 2) * 8, 8), 8), :]
    starts = jnp.zeros((8, 128), jnp.int32)
    for n in range(1, 16):
        begin = jnp.sum((docs < n).astype(jnp.int32))
        starts = jnp.where(half == n, begin, starts)
    row = lax.broadcasted_iota(jnp.int32, (8, 128), 0)
    lane = lax.broadcasted_iota(jnp.int32, (8, 128), 1)
    pos = (c // 2) * (2 * SHARD) + row * 128 + lane
    starts = jnp.maximum(starts, pos - (WINDOW - 1))
    starts = jnp.where(c % 2 == 0, starts, jnp.concatenate([starts[4:8], starts[0:4]], axis=0))
    for r in range(4):
        wide = jnp.broadcast_to(starts[r:r + 1, :], (128, 128))
        lower[pl.ds(r * 128, 128), :] = jnp.transpose(wide)
    oacc[...] = jnp.zeros_like(oacc)
    dacc[...] = jnp.zeros_like(dacc)

    for d in order:
        src = lax.rem(y - d + NY, NY)
        remote(wk.at[z, src], wk.at[z, src], k1s.at[d], k1r.at[d], at(z, y)).wait_recv()
        src = lax.rem(z - d + NZ, NZ)
        remote(wv.at[y, src], wv.at[y, src], v1s.at[d], v1r.at[d], at(z, y)).wait_recv()

    def ring(buf, ssem, rsem, me, towards, side, s, piece):
        sign = 1 - 2 * side
        src = lax.rem(me - sign * (s - 1) + 8, 8)
        part = pl.ds(4 * piece, 4)
        return remote(buf.at[src, part], buf.at[src, part], ssem.at[side, s, piece], rsem.at[side, s, piece], towards(sign))

    def along_z(sign):
        return at(z + sign, y)

    def along_y(sign):
        return at(z, y + sign)

    def arrived(buf, ssem, rsem, me, towards, side, s, piece):
        sign = 1 - 2 * side
        src = lax.rem(me - sign * s + 8, 8)
        part = pl.ds(4 * piece, 4)
        remote(buf.at[src, part], buf.at[src, part], ssem.at[side, s, piece], rsem.at[side, s, piece], towards(sign)).wait_recv()

    streams = ((wk, k2s, k2r, z, along_z), (wv, v2s, v2r, y, along_y))

    def steps_of(side, piece):
        return 4 if side == piece else 3

    for s in range(1, 5):
        for piece in (0, 1):
            for side in (0, 1):
                for st in streams:
                    last = steps_of(side, piece)
                    if s > 1 and s - 1 <= last:
                        arrived(*st, side, s - 1, piece)
                    if s <= last:
                        go(ring(*st, side, s, piece))
        q_first(s)
    q_first_done()

    def q_stage(h, s):
        for piece in (0, 1):
            for side in (1, 0):
                last = 4 if side == 1 else 3
                args = (wq.at[h], q2s.at[h], q2r.at[h], z, along_z, side)
                if s > 1 and s - 1 <= last:
                    arrived(*args, s - 1, piece)
                if s <= last:
                    go(ring(*args, s, piece))

    q_stage(0, 1)
    for piece in (0, 1):
        side = piece
        for st in streams:
            arrived(*st, side, 4, piece)

    own_tok.wait()
    acc[...] = jnp.zeros_like(acc)

    def kv_dot(i, carry):
        ws = []
        for zz in (0, 1):
            for yy in range(8):
                kk = wk[2 * i + zz, yy].astype(F32)
                vv = wv[yy, 2 * i + zz].astype(F32)
                ws.append(jnp.concatenate([kk, vv], axis=1))
        w = jnp.concatenate(ws, axis=0).astype(BF)
        t = tok[:, pl.ds(pl.multiple_of(i * 1152, 1152), 1152)]
        acc[...] += jnp.dot(t, w, preferred_element_type=F32)
        return carry

    lax.fori_loop(0, 4, kv_dot, 0)
    kvs[0] = acc[...].astype(BF)

    def reach(yy):
        yy = lax.rem(yy + NY, NY)
        return 3 + jnp.where(yy >= 4, 1, 0) + jnp.where(yy == 7, 1, 0) - jnp.where(yy == 0, 1, 0)

    mine, nxt, prv = reach(y), reach(y + 1), reach(y - 1)
    right = (lax.rem(jnp.where(y == 7, c + 1, c + 1) + 64, 64), f)
    left = (lax.rem(c - 1 + 64, 64), f)

    def halo(src_slot, dst_slot, piece, side, dev):
        part = pl.ds(256 * piece, 256)
        return remote(kvs.at[src_slot, part], kvs.at[dst_slot, part], hs.at[side, dst_slot, piece], hr.at[dst_slot, piece], dev)

    def halo_wait(slot, piece):
        halo(slot, slot, piece, 0, at(z, y)).wait_recv()

    for piece in (0, 1):
        part = pl.ds(256 * piece, 256)
        go(remote(kvs.at[0, part], kvs.at[8, part], hzs.at[piece], hr.at[8, piece], at(z + 1, y)))

        @pl.when(y != 7)
        def _():
            halo(0, 1, piece, 0, at(z, y + 1)).start()

        @pl.when(y == 0)
        def _():
            halo(0, 7, piece, 1, at(z, y - 1)).start()

    def halo_first():
        for piece in (0, 1):
            halo_wait(8, piece)

            @pl.when(y == 7)
            def _():
                halo(8, 1, piece, 0, at(z, y + 1)).start()

            @pl.when(y != 0)
            def _():
                halo(8, 7, piece, 1, at(z, y - 1)).start()

    def halo_right(slot, ok):
        for piece in (0, 1):
            @pl.when(ok)
            def _():
                halo_wait(slot, piece)

                @pl.when(slot + 1 <= nxt)
                def _():
                    halo(slot, slot + 1, piece, 0, right).start()

    def halo_left(slot, ok):
        for piece in (0, 1):
            @pl.when(ok)
            def _():
                halo_wait(slot, piece)

                @pl.when(9 - slot <= 7 - prv)
                def _():
                    halo(slot, slot - 1, piece, 1, left).start()

    slot_a = jnp.where(mine == 2, 5, 3)
    slot_b = jnp.where((mine == 3) | (mine == 4), 5, 4)
    slot_c = 12 - slot_a - slot_b

    lane_id = lax.broadcasted_iota(jnp.int32, (1, 128), 1)

    def attend(h, slot):
        base = (c - slot) * SHARD

        def tile(i, carry):
            rows = pl.ds(pl.multiple_of(i * 256, 256), 256)
            s = lax.dot_general(q[h, rows, :], kvs[slot, :, pl.ds(0, HD)],
                                (((1,), (1,)), ((), ())), preferred_element_type=F32)
            low = lower[rows, :] - base
            den = dacc[h, rows, :]
            parts = []
            for t in range(4):
                e = jnp.exp2(jnp.tanh(s[:, t * 128:(t + 1) * 128] * IN_SCALE) * OUT_SCALE)
                e = jnp.where(lane_id + t * 128 >= low, e, 0.0)
                den += e
                parts.append(e.astype(BF))
            dacc[h, rows, :] = den
            p = jnp.concatenate(parts, axis=1)
            oacc[h, rows, :] += jnp.dot(p, kvs[slot, :, pl.ds(HD, HD)], preferred_element_type=F32)
            return carry

        lax.fori_loop(0, 2, tile, 0)

    def attend_own(h):
        for i in range(4):
            n = i + 1
            rows = pl.ds(i * 128, 128)
            s = lax.dot_general(q[h, rows, :], kvs[0, pl.ds(0, n * 128), pl.ds(0, HD)],
                                (((1,), (1,)), ((), ())), preferred_element_type=F32)
            low = lower[rows, :] - c * SHARD
            den = dacc[h, rows, :]
            parts = []
            for t in range(n):
                e = jnp.exp2(jnp.tanh(s[:, t * 128:(t + 1) * 128] * IN_SCALE) * OUT_SCALE)
                seen = lane_id + t * 128 >= low
                if t == i:
                    seen = seen & (lane_id <= lax.broadcasted_iota(jnp.int32, (128, 128), 0))
                e = jnp.where(seen, e, 0.0)
                den += e
                parts.append(e.astype(BF))
            dacc[h, rows, :] = den
            p = jnp.concatenate(parts, axis=1) if n > 1 else parts[0]
            oacc[h, rows, :] += jnp.dot(p, kvs[0, pl.ds(0, n * 128), pl.ds(HD, HD)], preferred_element_type=F32)

    def q_dot(h):
        cols = pl.ds(0, HD)
        acc[:, cols] = jnp.zeros((SHARD, HD), F32)

        def step(i, carry):
            ws = []
            for zz in (0, 1):
                for yy in range(8):
                    ws.append(wq[h, 2 * i + zz, yy].astype(F32))
            w = jnp.concatenate(ws, axis=0).astype(BF)
            t = tok[:, pl.ds(pl.multiple_of(i * 1152, 1152), 1152)]
            acc[:, cols] += jnp.dot(t, w, preferred_element_type=F32)
            return carry

        lax.fori_loop(0, 4, step, 0)
        q[h] = acc[:, cols].astype(BF)

    def finish(h):
        den = jnp.sum(dacc[h], axis=1, keepdims=True)
        att[h] = (oacc[h] / den).astype(BF)
        for d in range(1, NF):
            peer = lax.rem(f + d, NF)
            rows = pl.ds(pl.multiple_of(peer * 64, 64), 64)
            cols = pl.ds(pl.multiple_of(f * 256 + h * HD, HD), HD)
            go(remote(att.at[h, rows], out_ref.at[:, cols], as_.at[h, d], ar.at[h, d], (c, peer)))
        rows = pl.ds(pl.multiple_of(f * 64, 64), 64)
        cols = pl.ds(pl.multiple_of(f * 256 + h * HD, HD), HD)
        pltpu.make_async_copy(att.at[h, rows], out_ref.at[:, cols], loc_sem.at[h]).start()

    def finish_wait(h):
        rows = pl.ds(pl.multiple_of(f * 64, 64), 64)
        for d in range(1, NF):
            peer = lax.rem(f - d + NF, NF)
            cols = pl.ds(pl.multiple_of(peer * 256 + h * HD, HD), HD)
            remote(att.at[h, rows], out_ref.at[:, cols], as_.at[h, d], ar.at[h, d], (c, f)).wait_recv()
        cols = pl.ds(pl.multiple_of(f * 256 + h * HD, HD), HD)
        pltpu.make_async_copy(att.at[h, rows], out_ref.at[:, cols], loc_sem.at[h]).wait()

    q_stage(0, 2)
    halo_first()
    halo_right(1, mine >= 1)
    q_stage(0, 3)
    q_stage(0, 4)
    q_stage(1, 1)
    halo_left(7, mine <= 6)
    halo_right(2, mine >= 2)
    q_stage(0, 5)
    q_dot(0)
    attend_own(0)
    q_stage(1, 2)
    attend(0, 8)
    attend(0, 1)
    halo_left(6, mine <= 5)
    halo_left(slot_a, mine == 2)
    halo_right(slot_a, mine != 2)
    q_stage(1, 3)
    lax.fori_loop(0, 3, lambda i, x: (attend(0, jnp.where(i == 0, 7, jnp.where(i == 1, 2, 6))), x)[1], 0)
    q_stage(1, 4)
    attend(0, slot_a)
    left_b = (mine <= 4)
    halo_left(slot_b, left_b)
    halo_right(slot_b, jnp.logical_not(left_b))
    attend(0, slot_b)
    q_stage(1, 5)
    q_dot(1)
    attend_own(1)

    def later(i, x):
        slot = jnp.where(i == 0, 8, jnp.where(i == 1, 1, jnp.where(i == 2, 7, jnp.where(
            i == 3, 2, jnp.where(i == 4, 6, jnp.where(i == 5, slot_a, slot_b))))))
        attend(1, slot)
        return x

    lax.fori_loop(0, 7, later, 0)
    left_c = (mine <= 3)
    halo_left(slot_c, left_c)
    halo_right(slot_c, jnp.logical_not(left_c))
    attend(0, slot_c)
    finish(0)
    attend(1, slot_c)
    finish(1)

    for copy in sent:
        copy.wait_send()
    for piece in (0, 1):
        halo(0, 1, piece, 0, right).wait_send()
        halo(0, 7, piece, 1, left).wait_send()
        for s in range(2, 6):
            @pl.when(s <= nxt)
            def _():
                halo(0, s, piece, 0, right).wait_send()

            @pl.when(s <= 7 - prv)
            def _():
                halo(0, 8 - s, piece, 1, left).wait_send()
    finish_wait(0)
    finish_wait(1)


def on_device(tokens, w_query, w_key, w_value, doc_ids):
    docs = doc_ids.reshape(256, 128)
    hbm = pl.BlockSpec(memory_space=pl.ANY)
    vmem = pl.BlockSpec(memory_space=pltpu.VMEM)
    dma = pltpu.SemaphoreType.DMA
    return pl.pallas_call(
        kernel,
        out_shape=jax.ShapeDtypeStruct((64, 2048), BF),
        in_specs=[hbm, hbm, hbm, hbm, vmem],
        out_specs=hbm,
        scratch_shapes=[
            pltpu.VMEM((SHARD, D), BF),
            pltpu.VMEM((8, 8, SLAB, HD), BF),
            pltpu.VMEM((8, 8, SLAB, HD), BF),
            pltpu.VMEM((2, 8, 8, SLAB, HD), BF),
            pltpu.VMEM((9, SHARD, 2 * HD), BF),
            pltpu.VMEM((2, SHARD, HD), BF),
            pltpu.VMEM((SHARD, 2 * HD), F32),
            pltpu.VMEM((2, SHARD, HD), F32),
            pltpu.VMEM((2, SHARD, HD), F32),
            pltpu.VMEM((SHARD, HD), jnp.int32),
            pltpu.VMEM((2, SHARD, HD), BF),
            dma((5,)),
            dma((8,)), dma((8,)), dma((8,)), dma((8,)),
            dma((2, 5, 2)), dma((2, 5, 2)), dma((2, 5, 2)), dma((2, 5, 2)),
            dma((2, 5)), dma((2, 5)),
            dma((2, 2, 5, 2)), dma((2, 2, 5, 2)),
            dma((2,)), dma((2, 9, 2)), dma((9, 2)),
            dma((2, 8)), dma((2, 8)),
        ],
        compiler_params=pltpu.CompilerParams(
            collective_id=0, has_side_effects=True, vmem_limit_bytes=48 << 20),
        cost_estimate=pl.CostEstimate(flops=5 * 10 ** 9, bytes_accessed=10 ** 7, transcendentals=9 * 10 ** 6),
    )(tokens, w_query, w_key, w_value, docs)


def solution(mesh):
    return jax.shard_map(
        on_device,
        mesh=mesh,
        in_specs=(P("ctx", None), P("ctx", "fsdp"), P("ctx", "fsdp"), P("ctx", "fsdp"), P()),
        out_specs=P(("ctx", "fsdp"), None),
        check_vma=False,
    )
```

time: 366 us -> 106 us (0.29)
  waiting for transfers between devices: 226 us -> 0 us
  Pallas kernels: 0 us -> 99.3 us
  matrix products: 40.7 us -> 0 us
  starting transfers between devices: 30.1 us -> 0 us
  local copies, waits for them, and re-layouts: 36.2 us -> 6.16 us
  blocking collectives: 14.7 us -> 0 us
  between operations: 13.3 us -> 0.01 us
  other arithmetic: 4.33 us -> 0 us
    all_gather x3 -> x0, waiting for transfers between devices: 197 us -> none  [the longest x1 81.5 us: on_device(): lax.all_gather(w_value, 'ctx', axis=0, tiled=True)]
    pallas_call x0 -> x1, Pallas kernels: none -> 99.3 us  [on_device(): pl.pallas_call(kernel, out_shape=jax.ShapeDtypeStruct((64, 2048), BF), in...]
    dot_general x21 -> x0, matrix products: 40.7 us -> none  [the longest x9 15.3 us: update(): jnp.einsum('cngd,lnd->ngcl', query_heads, key_tile, preferred_element_typ...]
    ppermute x8 -> x0, starting transfers between devices: 30 us -> none  [passed_along(): return lax.ppermute(shard, axis, pairs)]
    gather x9 -> x0, local copies, waits for them, and re-layouts: 28.7 us -> none  [tile_mask(): key_doc = jnp.take(doc_ids, jnp.clip(key_pos, 0, last_pos))]
    ppermute x8 -> x0, waiting for transfers between devices: 26.2 us -> none  [passed_along(): return lax.ppermute(shard, axis, pairs)]
    all_to_all x1 -> x0, blocking collectives: 14.7 us -> none  [on_device(): lax.all_to_all(head_results, 'fsdp', split_axis=0, concat_axis=1, tiled=T...]
    and x9 -> x0, other arithmetic: 3.71 us -> none  [tile_mask(): (query_doc[:, None] == key_doc[None, :]) & (distance >= 0)]
  transfers between devices with their start and end apart: 11 -> 0, of which waited for: 6 -> 0; matrix products, arithmetic and copies ran while one was open for 5% -> 0% of each run, Pallas kernels for 0% -> 0%
where the time goes in v1:
time: 106 us; the launch traced here: 105 us
  Pallas kernels  99.3 us (94%)
  local copies, waits for them, and re-layouts  6.16 us (6%)
    pallas_call x1, Pallas kernels, on_device(): pl.pallas_call(kernel, out_shape=jax.ShapeDtypeStruct((64, 2048), BF), in...  99.3 us
    unnamed x11, local copies, waits for them, and re-layouts  6.16 us

profile of v1, /device:TPU:1, one launch (start us, length us, event | category | flops | bytes accessed | tf_op | source)
XLA Modules:
  0.0 105.4 jit_solution(14523180530128971735)
XLA Ops:
  0.0 0.0 copy-start
  0.0 2.3 %copy-done = bf16[512,4608]{1,0:T(8,128)(2,1)S(1)} copy-done((bf16[512,4608]{1,0:T(8,128)(2,1)S(1)}, bf16[512,4608]{1,0:T(8,128)(2,1)}, u32[]{:S(2)}) %copy-start) | copy-done | bytes 4718616
  2.3 0.0 copy-start.1
  2.3 0.9 copy-done.1
  3.2 0.0 copy-start.2
  3.2 0.8 copy-done.2
  4.0 0.0 copy-start.3
  4.0 0.7 copy-done.3
  4.7 0.0 copy-start.4
  4.7 0.7 copy-done.4
  5.5 99.3 %shard_map.55 = bf16[64,2048]{1,0:T(8,128)(2,1)S(1)} custom-call(bf16[512,4608]{1,0:T(8,128)(2,1)S(1)} %copy-done, bf16[72,256]{1,0:T(8,128)(2,1)S(1)} %copy-done.2, bf16[72,128]{1,0:T(8,128)(2,1)S(1)} %copy-done.3, bf16[72,128]{1,0:T(8,128)(2,1)S(1)} %copy-done.4, s32[256,128]{1,0:T(8,128)S(1)} %bitcast.1), custom_call_target="tpu_custom_call" | custom-call | flops 5000000000 | bytes 10000000 | tf_op jit(solution)/shard_map/pallas_call | solution.py:408
  104.7 0.7 copy.7
Async XLA Ops:
  0.0 2.3 %copy-start = (bf16[512,4608]{1,0:T(8,128)(2,1)S(1)}, bf16[512,4608]{1,0:T(8,128)(2,1)}, u32[]{:S(2)}) copy-start(bf16[512,4608]{1,0:T(8,128)(2,1)} %tok_hbm.1) | copy-start | bytes 14155780
  2.3 0.9 copy-start.1
  3.2 0.8 copy-start.2
  4.0 0.7 copy-start.3
  4.7 0.7 copy-start.4

commit v2 on v1

v2 whole, which is shorter than its diff:
```python
import functools
import math

import jax
import jax.numpy as jnp
from jax import lax
from jax.experimental import pallas as pl
from jax.experimental.pallas import tpu as pltpu
from jax.sharding import PartitionSpec as P

MESH = pl.DeviceIdType.MESH
HD = 128
WINDOW = 4096
SHARD = 512
D = 4608
SLAB = 72
NZ = NY = 8
NF = 8
BF = jnp.bfloat16
F32 = jnp.float32

query_scale = 144.0 ** (-0.5)
score_cap = 50.0
IN_SCALE = query_scale / score_cap
OUT_SCALE = score_cap * math.log2(math.e)

ORDER = (
    ('S',), ('F', 1), ('F', 2), ('W',), ('K', 1, 1), ('F', 3), ('K', 1, 0), ('K', 2, 1), ('K', 2, 0),
    ('F', 4), ('K', 3, 1), ('K', 3, 0), ('G',), ('Q', 0, 1, 1), ('Q', 0, 1, 0), ('K', 4, 1), ('Q', 1, 1, 0),
    ('K', 4, 0), ('Q', 0, 2, 0), ('K', 5, 1), ('Q', 1, 1, 1), ('K', 5, 0), ('Q', 0, 2, 1), ('P',), ('B', 0),
    ('Q', 1, 2, 1), ('B', 1), ('Q', 0, 3, 0), ('H', 8, 0), ('Q', 0, 4, 0), ('Q', 0, 3, 1), ('Q', 1, 3, 1),
    ('Q', 1, 2, 0), ('D',), ('H', 8, 1), ('H', 1, 0), ('H', 7, 0), ('Q', 0, 4, 1), ('Q', 1, 4, 1),
    ('Q', 1, 3, 0), ('Q', 0, 5, 0), ('H', 7, 1), ('H', 1, 1), ('Q', 0, 5, 1), ('R', 0), ('O', 0),
    ('H', 6, 0), ('A', 0, 8), ('H', 2, 0), ('A', 0, 1), ('Q', 1, 4, 0), ('H', 6, 1), ('A', 0, 7),
    ('H', 2, 1), ('A', 0, 6), ('Q', 1, 5, 1), ('A', 0, 2), ('H', 3, 0), ('Q', 1, 5, 0), ('R', 1), ('O', 1),
    ('H', 5, 0), ('A', 1, 6), ('A', 1, 8), ('H', 3, 1), ('A', 1, 3), ('A', 1, 2), ('H', 4, 0), ('A', 1, 7),
    ('H', 5, 1), ('A', 1, 1), ('A', 1, 5), ('A', 0, 3), ('H', 4, 1), ('A', 1, 4), ('A', 0, 4), ('A', 0, 5),
)


def kernel(tok_hbm, wq_hbm, wk_hbm, wv_hbm, doc_hbm, out_ref,
           doc_ref, tok, wk, wv, wq, kvs, q, acc, oacc, dacc, lower, att,
           loc_sem, k1s, k1r, v1s, v1r, k2s, k2r, v2s, v2r, q1s, q1r, q2s, q2r,
           hs, hr, as_, ar):
    c = lax.axis_index("ctx")
    f = lax.axis_index("fsdp")
    z, y = c // NY, c % NY

    def at(zz, yy):
        return (lax.rem(zz + NZ, NZ) * NY + lax.rem(yy + NY, NY), f)

    def remote(src, dst, ssem, rsem, dev):
        return pltpu.make_async_remote_copy(
            src_ref=src, dst_ref=dst, send_sem=ssem, recv_sem=rsem,
            device_id=dev, device_id_type=MESH)

    sent = []

    def go(copy):
        copy.start()
        sent.append(copy)

    own_q0 = pltpu.make_async_copy(wq_hbm.at[:, pl.ds(0, HD)], wq.at[0, z, y], loc_sem.at[0])
    own_q1 = pltpu.make_async_copy(wq_hbm.at[:, pl.ds(HD, HD)], wq.at[1, z, y], loc_sem.at[1])
    own_k = pltpu.make_async_copy(wk_hbm, wk.at[z, y], loc_sem.at[2])
    own_v = pltpu.make_async_copy(wv_hbm, wv.at[y, z], loc_sem.at[3])
    own_doc = pltpu.make_async_copy(doc_hbm, doc_ref, loc_sem.at[5])
    own_tok = pltpu.make_async_copy(tok_hbm, tok, loc_sem.at[4])
    own_k.start()
    own_v.start()
    own_q0.start()
    own_q1.start()
    own_doc.start()
    own_tok.start()

    bar = pltpu.get_barrier_semaphore()
    peers = [at(z, y + d) for d in range(1, NY)]
    peers += [at(z + d, y) for d in range(1, NZ)]
    peers += [(c, lax.rem(f + d, NF)) for d in range(1, NF)]
    for p in peers:
        pl.semaphore_signal(bar, inc=1, device_id=p, device_id_type=MESH)

    @pl.when(y == NY - 1)
    def _():
        pl.semaphore_signal(bar, inc=1, device_id=at(z + 1, 0), device_id_type=MESH)

    @pl.when(y == 0)
    def _():
        pl.semaphore_signal(bar, inc=1, device_id=at(z - 1, NY - 1), device_id_type=MESH)

    edge = jnp.where((y == 0) | (y == NY - 1), 1, 0)
    pl.semaphore_wait(bar, len(peers) + edge)

    order = [1, 7, 2, 6, 3, 5, 4]

    def first_slabs():
        own_k.wait()
        own_v.wait()
        for d in order:
            go(remote(wk.at[z, y], wk.at[z, y], k1s.at[d], k1r.at[d], at(z, y + d)))
            go(remote(wv.at[y, z], wv.at[y, z], v1s.at[d], v1r.at[d], at(z + d, y)))
        own_q0.wait()
        own_q1.wait()
        oacc[...] = jnp.zeros_like(oacc)
        dacc[...] = jnp.zeros_like(dacc)

    def first_slabs_wait():
        for d in order:
            src = lax.rem(y - d + NY, NY)
            remote(wk.at[z, src], wk.at[z, src], k1s.at[d], k1r.at[d], at(z, y)).wait_recv()
            src = lax.rem(z - d + NZ, NZ)
            remote(wv.at[y, src], wv.at[y, src], v1s.at[d], v1r.at[d], at(z, y)).wait_recv()

    def q_first(s):
        for side in (0, 1):
            sign = 1 - 2 * side
            if s > (4 if side == 0 else 3):
                continue
            src = lax.rem(y - sign * (s - 1) + NY, NY)
            if s > 1:
                remote(wq.at[:, z, src], wq.at[:, z, src], q1s.at[side, s - 1], q1r.at[side, s - 1], at(z, y)).wait_recv()
            go(remote(wq.at[:, z, src], wq.at[:, z, src], q1s.at[side, s], q1r.at[side, s], at(z, y + sign)))

    def q_first_done():
        for side, s in ((0, 4), (1, 3)):
            sign = 1 - 2 * side
            src = lax.rem(y - sign * s + NY, NY)
            remote(wq.at[:, z, src], wq.at[:, z, src], q1s.at[side, s], q1r.at[side, s], at(z, y)).wait_recv()

    def bounds():
        own_doc.wait()
        docs = doc_ref[...]
        half = doc_ref[pl.ds(pl.multiple_of((c // 2) * 8, 8), 8), :]
        starts = jnp.zeros((8, 128), jnp.int32)
        for n in range(1, 16):
            begin = jnp.sum((docs < n).astype(jnp.int32))
            starts = jnp.where(half == n, begin, starts)
        row = lax.broadcasted_iota(jnp.int32, (8, 128), 0)
        lane = lax.broadcasted_iota(jnp.int32, (8, 128), 1)
        pos = (c // 2) * (2 * SHARD) + row * 128 + lane
        starts = jnp.maximum(starts, pos - (WINDOW - 1))
        starts = jnp.where(c % 2 == 0, starts, jnp.concatenate([starts[4:8], starts[0:4]], axis=0))
        for r in range(4):
            wide = jnp.broadcast_to(starts[r:r + 1, :], (128, 128))
            lower[pl.ds(r * 128, 128), :] = jnp.transpose(wide)

    def ring(buf, ssem, rsem, me, towards, side, s, piece):
        sign = 1 - 2 * side
        src = lax.rem(me - sign * (s - 1) + 8, 8)
        part = pl.ds(4 * piece, 4)
        return remote(buf.at[src, part], buf.at[src, part], ssem.at[side, s, piece], rsem.at[side, s, piece], towards(sign))

    def along_z(sign):
        return at(z + sign, y)

    def along_y(sign):
        return at(z, y + sign)

    def ring_step(stream, side, s, piece, last):
        buf, ssem, rsem, me, towards = stream
        sign = 1 - 2 * side
        if s > 1 and s - 1 <= last:
            src = lax.rem(me - sign * (s - 1) + 8, 8)
            part = pl.ds(4 * piece, 4)
            remote(buf.at[src, part], buf.at[src, part], ssem.at[side, s - 1, piece],
                   rsem.at[side, s - 1, piece], towards(sign)).wait_recv()
        if s <= last:
            go(ring(*stream, side, s, piece))

    def kv_step(s, piece):
        for side in (0, 1):
            for stream in ((wk, k2s, k2r, z, along_z), (wv, v2s, v2r, y, along_y)):
                ring_step(stream, side, s, piece, 4 if side == piece else 3)

    def q_step(h, s, piece):
        for side in (1, 0):
            ring_step((wq.at[h], q2s.at[h], q2r.at[h], z, along_z), side, s, piece, 4 if side == 1 else 3)

    def kv_project():
        own_tok.wait()
        acc[...] = jnp.zeros_like(acc)

        def kv_dot(i, carry):
            ws = []
            for zz in (0, 1):
                for yy in range(8):
                    kk = wk[2 * i + zz, yy].astype(F32)
                    vv = wv[yy, 2 * i + zz].astype(F32)
                    ws.append(jnp.concatenate([kk, vv], axis=1))
            w = jnp.concatenate(ws, axis=0).astype(BF)
            t = tok[:, pl.ds(pl.multiple_of(i * 1152, 1152), 1152)]
            acc[...] += jnp.dot(t, w, preferred_element_type=F32)
            return carry

        lax.fori_loop(0, 4, kv_dot, 0)
        kvs[0] = acc[...].astype(BF)

    right = (lax.rem(c + 1, 64), f)
    left = (lax.rem(c + 63, 64), f)

    def halo(src_slot, dst_slot, piece, dev, extra=False):
        part = pl.ds(256 * piece, 256)
        return remote(kvs.at[src_slot, part], kvs.at[dst_slot, part], hs.at[0 if extra else dst_slot, piece],
                      hr.at[dst_slot, piece], dev)

    def halo_start(piece):
        go(halo(0, 8, piece, at(z + 1, y)))

        @pl.when(y != 7)
        def _():
            halo(0, 1, piece, at(z, y + 1)).start()

        @pl.when(y == 0)
        def _():
            halo(0, 7, piece, at(z, y - 1)).start()

    def halo_step(slot, piece):
        halo(slot, slot, piece, at(z, y)).wait_recv()
        if slot == 8:
            @pl.when(y == 7)
            def _():
                halo(8, 1, piece, at(z, y + 1)).start()

            @pl.when(y != 0)
            def _():
                halo(8, 7, piece, at(z, y - 1)).start()
        elif slot < 3:
            go(halo(slot, slot + 1, piece, right))
        elif slot == 3:
            @pl.when(y != 7)
            def _():
                halo(3, 4, piece, right).start()
        elif slot == 4:
            @pl.when(y == 6)
            def _():
                halo(4, 5, piece, right, True).start()
        elif slot == 5:
            @pl.when(y == 1)
            def _():
                halo(5, 4, piece, left, True).start()
        elif slot == 6:
            @pl.when(y != 0)
            def _():
                halo(6, 5, piece, left).start()
        else:
            go(halo(slot, slot - 1, piece, left))

    def halo_end():
        for piece in (0, 1):
            halo(0, 1, piece, right).wait_send()
            halo(0, 7, piece, left).wait_send()

            @pl.when(y != 7)
            def _():
                halo(0, 4, piece, right).wait_send()

            @pl.when(y != 0)
            def _():
                halo(0, 5, piece, left).wait_send()

            @pl.when((y == 1) | (y == 6))
            def _():
                halo(0, 4, piece, left, True).wait_send()

    lane_id = lax.broadcasted_iota(jnp.int32, (1, 128), 1)

    def attend(h, slot):
        base = (c - slot) * SHARD

        def tile(rows):
            s = lax.dot_general(q[h, rows, :], kvs[slot, :, pl.ds(0, HD)],
                                (((1,), (1,)), ((), ())), preferred_element_type=F32)
            low = lower[rows, :] - base
            den = dacc[h, rows, :]
            parts = []
            for t in range(4):
                e = jnp.exp2(jnp.tanh(s[:, t * 128:(t + 1) * 128] * IN_SCALE) * OUT_SCALE)
                e = jnp.where(lane_id + t * 128 >= low, e, 0.0)
                den += e
                parts.append(e.astype(BF))
            dacc[h, rows, :] = den
            p = jnp.concatenate(parts, axis=1)
            oacc[h, rows, :] += jnp.dot(p, kvs[slot, :, pl.ds(HD, HD)], preferred_element_type=F32)

        tile(pl.ds(0, SHARD))

    def attend_own(h):
        for i in range(4):
            n = i + 1
            rows = pl.ds(i * 128, 128)
            s = lax.dot_general(q[h, rows, :], kvs[0, pl.ds(0, n * 128), pl.ds(0, HD)],
                                (((1,), (1,)), ((), ())), preferred_element_type=F32)
            low = lower[rows, :] - c * SHARD
            den = dacc[h, rows, :]
            parts = []
            for t in range(n):
                e = jnp.exp2(jnp.tanh(s[:, t * 128:(t + 1) * 128] * IN_SCALE) * OUT_SCALE)
                seen = lane_id + t * 128 >= low
                if t == i:
                    seen = seen & (lane_id <= lax.broadcasted_iota(jnp.int32, (128, 128), 0))
                e = jnp.where(seen, e, 0.0)
                den += e
                parts.append(e.astype(BF))
            dacc[h, rows, :] = den
            p = jnp.concatenate(parts, axis=1) if n > 1 else parts[0]
            oacc[h, rows, :] += jnp.dot(p, kvs[0, pl.ds(0, n * 128), pl.ds(HD, HD)], preferred_element_type=F32)

    def q_dot(h):
        cols = pl.ds(0, HD)
        acc[:, cols] = jnp.zeros((SHARD, HD), F32)

        def step(i, carry):
            ws = []
            for zz in (0, 1):
                for yy in range(8):
                    ws.append(wq[h, 2 * i + zz, yy].astype(F32))
            w = jnp.concatenate(ws, axis=0).astype(BF)
            t = tok[:, pl.ds(pl.multiple_of(i * 1152, 1152), 1152)]
            acc[:, cols] += jnp.dot(t, w, preferred_element_type=F32)
            return carry

        lax.fori_loop(0, 4, step, 0)
        q[h] = acc[:, cols].astype(BF)

    def finish(h):
        den = jnp.sum(dacc[h], axis=1, keepdims=True)
        att[h] = (oacc[h] / den).astype(BF)
        for d in range(1, NF):
            peer = lax.rem(f + d, NF)
            rows = pl.ds(pl.multiple_of(peer * 64, 64), 64)
            cols = pl.ds(pl.multiple_of(f * 256 + h * HD, HD), HD)
            go(remote(att.at[h, rows], out_ref.at[:, cols], as_.at[h, d], ar.at[h, d], (c, peer)))
        rows = pl.ds(pl.multiple_of(f * 64, 64), 64)
        cols = pl.ds(pl.multiple_of(f * 256 + h * HD, HD), HD)
        pltpu.make_async_copy(att.at[h, rows], out_ref.at[:, cols], loc_sem.at[h]).start()

    def finish_wait(h):
        rows = pl.ds(pl.multiple_of(f * 64, 64), 64)
        for d in range(1, NF):
            peer = lax.rem(f - d + NF, NF)
            cols = pl.ds(pl.multiple_of(peer * 256 + h * HD, HD), HD)
            remote(att.at[h, rows], out_ref.at[:, cols], as_.at[h, d], ar.at[h, d], (c, f)).wait_recv()
        cols = pl.ds(pl.multiple_of(f * 256 + h * HD, HD), HD)
        pltpu.make_async_copy(att.at[h, rows], out_ref.at[:, cols], loc_sem.at[h]).wait()

    def attend_run(run):
        if len(run) == 1:
            attend(*run[0])
            return

        def pick(i, values):
            value = values[-1]
            for n in range(len(values) - 1):
                value = jnp.where(i == n, values[n], value)
            return value

        def step(i, x):
            attend(pick(i, [h for h, _ in run]), pick(i, [slot for _, slot in run]))
            return x

        lax.fori_loop(0, len(run), step, 0)

    steps = {"S": first_slabs, "W": first_slabs_wait, "F": q_first, "G": q_first_done, "K": kv_step,
             "Q": q_step, "D": bounds, "P": kv_project, "B": halo_start, "H": halo_step,
             "R": q_dot, "O": attend_own}
    left_of = {h: sum(t[:2] == ("A", h) for t in ORDER) for h in (0, 1)}
    i = 0
    while i < len(ORDER):
        name, *args = ORDER[i]
        if name != "A":
            steps[name](*args)
            i += 1
            continue
        run = []
        while i < len(ORDER) and ORDER[i][0] == "A" and all(left_of.values()) | (not run):
            run.append(ORDER[i][1:])
            left_of[ORDER[i][1]] -= 1
            i += 1
        attend_run(run)
        for h in (0, 1):
            if left_of[h] == 0 and any(a == h for a, _ in run):
                finish(h)

    for copy in sent:
        copy.wait_send()
    halo_end()
    finish_wait(0)
    finish_wait(1)


def on_device(tokens, w_query, w_key, w_value, doc_ids):
    docs = doc_ids.reshape(256, 128)
    hbm = pl.BlockSpec(memory_space=pl.ANY)
    dma = pltpu.SemaphoreType.DMA
    return pl.pallas_call(
        kernel,
        out_shape=jax.ShapeDtypeStruct((64, 2048), BF),
        in_specs=[hbm] * 5,
        out_specs=hbm,
        scratch_shapes=[
            pltpu.VMEM((256, 128), jnp.int32),
            pltpu.VMEM((SHARD, D), BF),
            pltpu.VMEM((8, 8, SLAB, HD), BF),
            pltpu.VMEM((8, 8, SLAB, HD), BF),
            pltpu.VMEM((2, 8, 8, SLAB, HD), BF),
            pltpu.VMEM((9, SHARD, 2 * HD), BF),
            pltpu.VMEM((2, SHARD, HD), BF),
            pltpu.VMEM((SHARD, 2 * HD), F32),
            pltpu.VMEM((2, SHARD, HD), F32),
            pltpu.VMEM((2, SHARD, HD), F32),
            pltpu.VMEM((SHARD, HD), jnp.int32),
            pltpu.VMEM((2, SHARD, HD), BF),
            dma((6,)),
            dma((8,)), dma((8,)), dma((8,)), dma((8,)),
            dma((2, 5, 2)), dma((2, 5, 2)), dma((2, 5, 2)), dma((2, 5, 2)),
            dma((2, 5)), dma((2, 5)),
            dma((2, 2, 5, 2)), dma((2, 2, 5, 2)),
            dma((9, 2)), dma((9, 2)),
            dma((2, 8)), dma((2, 8)),
        ],
        compiler_params=pltpu.CompilerParams(
            collective_id=0, has_side_effects=True, vmem_limit_bytes=63 << 20),
        cost_estimate=pl.CostEstimate(flops=5 * 10 ** 9, bytes_accessed=10 ** 7, transcendentals=9 * 10 ** 6),
    )(tokens, w_query, w_key, w_value, docs)


def solution(mesh):
    return jax.shard_map(
        on_device,
        mesh=mesh,
        in_specs=(P("ctx", None), P("ctx", "fsdp"), P("ctx", "fsdp"), P("ctx", "fsdp"), P()),
        out_specs=P(("ctx", "fsdp"), None),
        check_vma=False,
    )
```

time: 106 us -> 95 us (0.90)
  Pallas kernels: 99.3 us -> 93.2 us
  local copies, waits for them, and re-layouts: 6.16 us -> 1.67 us
    pallas_call x1, Pallas kernels: 99.3 us -> 93.2 us  [on_device(): pl.pallas_call(kernel, out_shape=jax.ShapeDtypeStruct((64, 2048), BF), in...]
    unnamed x11 -> x1, local copies, waits for them, and re-layouts: 6.16 us -> 1.67 us
where the time goes in v2:
time: 95 us; the launch traced here: 94.9 us
  Pallas kernels  93.2 us (98%)
  local copies, waits for them, and re-layouts  1.67 us (2%)
    pallas_call x1, Pallas kernels, on_device(): pl.pallas_call(kernel, out_shape=jax.ShapeDtypeStruct((64, 2048), BF), in...  93.2 us

profile of v2, /device:TPU:1, one launch (start us, length us, event | category | flops | bytes accessed | tf_op | source)
XLA Modules:
  0.0 94.9 jit_solution(14966351551704236937)
XLA Ops:
  0.0 93.2 %shard_map.55 = bf16[64,2048]{1,0:T(8,128)(2,1)} custom-call(bf16[512,4608]{1,0:T(8,128)(2,1)} %tok_hbm.1, bf16[72,256]{1,0:T(8,128)(2,1)} %wq_hbm.1, bf16[72,128]{1,0:T(8,128)(2,1)} %wk_hbm.1, bf16[72,128]{1,0:T(8,128)(2,1)} %wv_hbm.1, s32[256,128]{1,0:T(8,128)} %bitcast.1), custom_call_target="tpu_custom_call" | custom-call | flops 5000000000 | bytes 10000000 | tf_op jit(solution)/shard_map/pallas_call | solution.py:395
  93.2 1.7 %copy.7 = bf16[64,2048]{1,0:T(8,128)(2,1)} copy(bf16[64,2048]{1,0:T(8,128)(2,1)} %shard_map.55) | data formatting | bytes 524288

commit v3 on v2

--- a/solution.py
+++ b/solution.py
@@ -12,6 +12,8 @@
 HD = 128
 WINDOW = 4096
 SHARD = 512
+K_PIECES, Q_PIECES, H_PIECES = 2, 2, 4
+H_ROWS = SHARD // H_PIECES
 D = 4608
 SLAB = 72
 NZ = NY = 8
@@ -25,16 +27,29 @@
 OUT_SCALE = score_cap * math.log2(math.e)
 
 ORDER = (
-    ('S',), ('F', 1), ('F', 2), ('W',), ('K', 1, 1), ('F', 3), ('K', 1, 0), ('K', 2, 1), ('K', 2, 0),
-    ('F', 4), ('K', 3, 1), ('K', 3, 0), ('G',), ('Q', 0, 1, 1), ('Q', 0, 1, 0), ('K', 4, 1), ('Q', 1, 1, 0),
-    ('K', 4, 0), ('Q', 0, 2, 0), ('K', 5, 1), ('Q', 1, 1, 1), ('K', 5, 0), ('Q', 0, 2, 1), ('P',), ('B', 0),
-    ('Q', 1, 2, 1), ('B', 1), ('Q', 0, 3, 0), ('H', 8, 0), ('Q', 0, 4, 0), ('Q', 0, 3, 1), ('Q', 1, 3, 1),
-    ('Q', 1, 2, 0), ('D',), ('H', 8, 1), ('H', 1, 0), ('H', 7, 0), ('Q', 0, 4, 1), ('Q', 1, 4, 1),
-    ('Q', 1, 3, 0), ('Q', 0, 5, 0), ('H', 7, 1), ('H', 1, 1), ('Q', 0, 5, 1), ('R', 0), ('O', 0),
-    ('H', 6, 0), ('A', 0, 8), ('H', 2, 0), ('A', 0, 1), ('Q', 1, 4, 0), ('H', 6, 1), ('A', 0, 7),
-    ('H', 2, 1), ('A', 0, 6), ('Q', 1, 5, 1), ('A', 0, 2), ('H', 3, 0), ('Q', 1, 5, 0), ('R', 1), ('O', 1),
-    ('H', 5, 0), ('A', 1, 6), ('A', 1, 8), ('H', 3, 1), ('A', 1, 3), ('A', 1, 2), ('H', 4, 0), ('A', 1, 7),
-    ('H', 5, 1), ('A', 1, 1), ('A', 1, 5), ('A', 0, 3), ('H', 4, 1), ('A', 1, 4), ('A', 0, 4), ('A', 0, 5),
+    ('S',), ('F', 1, 0), ('F', 1, 1), ('F', 2, 0), ('F', 2, 1), ('W',), ('K', 1, 1, 0, 0), ('K', 1, 1, 0, 1),
+    ('K', 1, 1, 1, 0), ('K', 1, 1, 1, 1), ('F', 3, 0), ('F', 3, 1), ('K', 1, 0, 0, 0), ('K', 1, 0, 0, 1),
+    ('K', 1, 0, 1, 0), ('K', 1, 0, 1, 1), ('K', 2, 1, 0, 0), ('K', 2, 1, 0, 1), ('K', 2, 1, 1, 0),
+    ('K', 2, 1, 1, 1), ('K', 2, 0, 0, 0), ('K', 2, 0, 0, 1), ('K', 2, 0, 1, 0), ('K', 2, 0, 1, 1),
+    ('F', 4, 0), ('K', 3, 1, 0, 0), ('K', 3, 1, 0, 1), ('K', 3, 1, 1, 0), ('K', 3, 1, 1, 1),
+    ('K', 3, 0, 0, 0), ('K', 3, 0, 0, 1), ('K', 3, 0, 1, 0), ('K', 3, 0, 1, 1), ('G',), ('Q', 0, 1, 1, 1),
+    ('Q', 0, 1, 1, 0), ('Q', 0, 1, 0, 1), ('Q', 0, 1, 0, 0), ('K', 4, 1, 0, 0), ('K', 4, 1, 0, 1),
+    ('K', 4, 1, 1, 0), ('K', 4, 1, 1, 1), ('Q', 1, 1, 0, 1), ('Q', 1, 1, 0, 0), ('K', 4, 0, 0, 0),
+    ('K', 4, 0, 0, 1), ('K', 4, 0, 1, 0), ('K', 4, 0, 1, 1), ('Q', 0, 2, 0, 1), ('Q', 0, 2, 0, 0),
+    ('K', 5, 1, 1, 0), ('K', 5, 1, 1, 1), ('Q', 1, 1, 1, 1), ('Q', 1, 1, 1, 0), ('K', 5, 0, 0, 0),
+    ('K', 5, 0, 0, 1), ('Q', 0, 2, 1, 1), ('Q', 0, 2, 1, 0), ('P',), ('B', 0), ('B', 1), ('Q', 1, 2, 1, 1),
+    ('Q', 1, 2, 1, 0), ('B', 2), ('B', 3), ('Q', 0, 3, 0, 1), ('Q', 0, 3, 0, 0), ('H', 8, 0), ('H', 8, 1),
+    ('Q', 0, 4, 0, 1), ('Q', 0, 4, 0, 0), ('Q', 0, 3, 1, 1), ('Q', 0, 3, 1, 0), ('Q', 1, 3, 1, 1),
+    ('Q', 1, 3, 1, 0), ('Q', 1, 2, 0, 1), ('Q', 1, 2, 0, 0), ('D',), ('H', 8, 2), ('H', 8, 3), ('H', 1, 0),
+    ('H', 1, 1), ('H', 7, 0), ('H', 7, 1), ('Q', 0, 4, 1, 1), ('Q', 0, 4, 1, 0), ('Q', 1, 4, 1, 1),
+    ('Q', 1, 4, 1, 0), ('Q', 1, 3, 0, 1), ('Q', 1, 3, 0, 0), ('Q', 0, 5, 0, 1), ('H', 7, 2), ('H', 7, 3),
+    ('H', 1, 2), ('H', 1, 3), ('Q', 0, 5, 1, 1), ('R', 0), ('O', 0), ('H', 6, 0), ('H', 6, 1), ('A', 0, 8),
+    ('H', 2, 0), ('H', 2, 1), ('A', 0, 1), ('Q', 1, 4, 0, 1), ('Q', 1, 4, 0, 0), ('H', 6, 2), ('H', 6, 3),
+    ('A', 0, 7), ('H', 2, 2), ('H', 2, 3), ('A', 0, 6), ('Q', 1, 5, 1, 1), ('A', 0, 2), ('H', 3, 0),
+    ('H', 3, 1), ('Q', 1, 5, 0, 1), ('R', 1), ('O', 1), ('H', 5, 0), ('H', 5, 1), ('A', 1, 6), ('A', 1, 8),
+    ('H', 3, 2), ('H', 3, 3), ('A', 1, 3), ('A', 1, 2), ('H', 4, 0), ('H', 4, 1), ('A', 1, 7), ('H', 5, 2),
+    ('H', 5, 3), ('A', 1, 1), ('A', 1, 5), ('A', 0, 3), ('H', 4, 2), ('H', 4, 3), ('A', 1, 4), ('A', 0, 4),
+    ('A', 0, 5),
 )
 
 
@@ -111,15 +126,12 @@
             src = lax.rem(z - d + NZ, NZ)
             remote(wv.at[y, src], wv.at[y, src], v1s.at[d], v1r.at[d], at(z, y)).wait_recv()
 
-    def q_first(s):
-        for side in (0, 1):
-            sign = 1 - 2 * side
-            if s > (4 if side == 0 else 3):
-                continue
-            src = lax.rem(y - sign * (s - 1) + NY, NY)
-            if s > 1:
-                remote(wq.at[:, z, src], wq.at[:, z, src], q1s.at[side, s - 1], q1r.at[side, s - 1], at(z, y)).wait_recv()
-            go(remote(wq.at[:, z, src], wq.at[:, z, src], q1s.at[side, s], q1r.at[side, s], at(z, y + sign)))
+    def q_first(s, side):
+        sign = 1 - 2 * side
+        src = lax.rem(y - sign * (s - 1) + NY, NY)
+        if s > 1:
+            remote(wq.at[:, z, src], wq.at[:, z, src], q1s.at[side, s - 1], q1r.at[side, s - 1], at(z, y)).wait_recv()
+        go(remote(wq.at[:, z, src], wq.at[:, z, src], q1s.at[side, s], q1r.at[side, s], at(z, y + sign)))
 
     def q_first_done():
         for side, s in ((0, 4), (1, 3)):
@@ -144,37 +156,32 @@
             wide = jnp.broadcast_to(starts[r:r + 1, :], (128, 128))
             lower[pl.ds(r * 128, 128), :] = jnp.transpose(wide)
 
-    def ring(buf, ssem, rsem, me, towards, side, s, piece):
-        sign = 1 - 2 * side
-        src = lax.rem(me - sign * (s - 1) + 8, 8)
-        part = pl.ds(4 * piece, 4)
-        return remote(buf.at[src, part], buf.at[src, part], ssem.at[side, s, piece], rsem.at[side, s, piece], towards(sign))
-
     def along_z(sign):
         return at(z + sign, y)
 
     def along_y(sign):
         return at(z, y + sign)
 
-    def ring_step(stream, side, s, piece, last):
+    def ring_step(stream, pieces, side, s, piece, last):
         buf, ssem, rsem, me, towards = stream
         sign = 1 - 2 * side
-        if s > 1 and s - 1 <= last:
+        part = pl.ds(8 // pieces * piece, 8 // pieces)
+        if s > 1:
             src = lax.rem(me - sign * (s - 1) + 8, 8)
-            part = pl.ds(4 * piece, 4)
             remote(buf.at[src, part], buf.at[src, part], ssem.at[side, s - 1, piece],
                    rsem.at[side, s - 1, piece], towards(sign)).wait_recv()
         if s <= last:
-            go(ring(*stream, side, s, piece))
-
-    def kv_step(s, piece):
-        for side in (0, 1):
-            for stream in ((wk, k2s, k2r, z, along_z), (wv, v2s, v2r, y, along_y)):
-                ring_step(stream, side, s, piece, 4 if side == piece else 3)
-
-    def q_step(h, s, piece):
-        for side in (1, 0):
-            ring_step((wq.at[h], q2s.at[h], q2r.at[h], z, along_z), side, s, piece, 4 if side == 1 else 3)
+            src = lax.rem(me - sign * (s - 1) + 8, 8)
+            go(remote(buf.at[src, part], buf.at[src, part], ssem.at[side, s, piece],
+                      rsem.at[side, s, piece], towards(sign)))
+
+    def kv_step(s, piece, side, stream):
+        last = 4 if (side == 0) == (piece < K_PIECES // 2) else 3
+        streams = ((wk, k2s, k2r, z, along_z), (wv, v2s, v2r, y, along_y))
+        ring_step(streams[stream], K_PIECES, side, s, piece, last)
+
+    def q_step(h, s, piece, side):
+        ring_step((wq.at[h], q2s.at[h], q2r.at[h], z, along_z), Q_PIECES, side, s, piece, 4 if side == 1 else 3)
 
     def kv_project():
         own_tok.wait()
@@ -199,7 +206,7 @@
     left = (lax.rem(c + 63, 64), f)
 
     def halo(src_slot, dst_slot, piece, dev, extra=False):
-        part = pl.ds(256 * piece, 256)
+        part = pl.ds(H_ROWS * piece, H_ROWS)
         return remote(kvs.at[src_slot, part], kvs.at[dst_slot, part], hs.at[0 if extra else dst_slot, piece],
                       hr.at[dst_slot, piece], dev)
 
@@ -246,7 +253,7 @@
             go(halo(slot, slot - 1, piece, left))
 
     def halo_end():
-        for piece in (0, 1):
+        for piece in range(H_PIECES):
             halo(0, 1, piece, right).wait_send()
             halo(0, 7, piece, left).wait_send()
 
@@ -367,6 +374,9 @@
     i = 0
     while i < len(ORDER):
         name, *args = ORDER[i]
+        if name == "H" and args[0] in (1, 2, 3) and args[1] == H_PIECES - 1:
+            while len(sent) > 40:
+                sent.pop(0).wait_send()
         if name != "A":
             steps[name](*args)
             i += 1
@@ -412,10 +422,10 @@
             pltpu.VMEM((2, SHARD, HD), BF),
             dma((6,)),
             dma((8,)), dma((8,)), dma((8,)), dma((8,)),
-            dma((2, 5, 2)), dma((2, 5, 2)), dma((2, 5, 2)), dma((2, 5, 2)),
+            dma((2, 5, K_PIECES)), dma((2, 5, K_PIECES)), dma((2, 5, K_PIECES)), dma((2, 5, K_PIECES)),
             dma((2, 5)), dma((2, 5)),
-            dma((2, 2, 5, 2)), dma((2, 2, 5, 2)),
-            dma((9, 2)), dma((9, 2)),
+            dma((2, 2, 5, Q_PIECES)), dma((2, 2, 5, Q_PIECES)),
+            dma((9, H_PIECES)), dma((9, H_PIECES)),
             dma((2, 8)), dma((2, 8)),
         ],
         compiler_params=pltpu.CompilerParams(

time: 95 us -> 94.7 us (level)
  no operation moved by 1% of the time
where the time goes in v3:
time: 94.7 us; the launch traced here: 94.2 us
  Pallas kernels  92.5 us (98%)
  local copies, waits for them, and re-layouts  1.67 us (2%)
    pallas_call x1, Pallas kernels, on_device(): pl.pallas_call(kernel, out_shape=jax.ShapeDtypeStruct((64, 2048), BF), in...  92.5 us

profile of v3, /device:TPU:1, one launch (start us, length us, event | category | flops | bytes accessed | tf_op | source)
XLA Modules:
  0.0 94.2 jit_solution(1349498550195525600)
XLA Ops:
  0.0 92.5 %shard_map.55 = bf16[64,2048]{1,0:T(8,128)(2,1)} custom-call(bf16[512,4608]{1,0:T(8,128)(2,1)} %tok_hbm.1, bf16[72,256]{1,0:T(8,128)(2,1)} %wq_hbm.1, bf16[72,128]{1,0:T(8,128)(2,1)} %wk_hbm.1, bf16[72,128]{1,0:T(8,128)(2,1)} %wv_hbm.1, s32[256,128]{1,0:T(8,128)} %bitcast.1), custom_call_target="tpu_custom_call" | custom-call | flops 5000000000 | bytes 10000000 | tf_op jit(solution)/shard_map/pallas_call | solution.py:405
  92.5 1.7 %copy.7 = bf16[64,2048]{1,0:T(8,128)(2,1)} copy(bf16[64,2048]{1,0:T(8,128)(2,1)} %shard_map.55) | data formatting | bytes 524288
